TPU v7x, 128 devices: a whole 4x4x4 slice. The times are simulated.
128 devices in a mesh: row: 8 (over x_lo, y), col: 16 (over z, x_hi, core).
Axes of the slice: x: 4 (x_hi: 2, x_lo: 2; x = x_hi * 2 + x_lo), y: 4, z: 4, core: 2. Of those that a mesh axis runs over, the one named last changes fastest.
Arguments:
- pair: bfloat16 [512, 512, 128], P('row', 'col'), may hold values from -6 to 6
- chain_id: int32 [512], replicated, may hold values from 0 to 3, never falling along the last dimension, each value on 1 to 256 neighbouring positions
- block_mask: int32 [8, 8], replicated, may hold values 0 or 1
- norm_gains: float32 [5, 128], replicated, may hold values from 0.1 to 1.9
- mult_in_weights: bfloat16 [2, 128, 640], replicated, may hold values from -0.5 to 0.5
- mult_out_weights: bfloat16 [2, 128, 128], replicated, may hold values from -0.5 to 0.5
- attn_weights: bfloat16 [128, 512], replicated, may hold values from -0.5 to 0.5
- bias_weights: bfloat16 [128, 4], replicated, may hold values from -0.5 to 0.5
- attn_out_weights: bfloat16 [128, 128], replicated, may hold values from -0.5 to 0.5
Outputs:
- pair_out: bfloat16 [512, 512, 128], P('row', 'col')
Inputs may be any that keep to these rules, and one draw needn't show every extreme that they name: `chain_id`: chains are runs of consecutive tokens; one chain holds exactly 256 tokens.
All inputs are finite; a program needn't handle non-finite values.
Results may differ from a plain program's by a relative error of at most 0.025.
Values may be sent and summed in bfloat16 or wider, within the bound.
A program may use at most 128 MiB of HBM per device.

v0:
```python
import math

import jax
import jax.numpy as jnp
from jax import lax
from jax.sharding import PartitionSpec as P

BLK = 64


def from_root(value, axis, source):
    kept = jnp.where(lax.axis_index(axis) == source, value, 0).astype(value.dtype)
    return lax.psum(kept, axis)


def layer_norm(values, gain):
    center = values - jnp.mean(values, axis=-1, keepdims=True)
    spread = jnp.mean(center * center, axis=-1, keepdims=True)
    return center * lax.rsqrt(spread + 1e-05) * gain


def allowed_pairs(chain_id, block_mask, row_first, row_count, col_first, col_count, block_size):
    row_chain = lax.dynamic_slice_in_dim(chain_id, row_first, row_count)
    col_chain = lax.dynamic_slice_in_dim(chain_id, col_first, col_count)
    same_chain = row_chain[:, None] == col_chain[None, :]
    blocks = block_mask.shape[0]
    block_ids = jnp.arange(blocks, dtype=jnp.int32)
    row_block = (row_first + jnp.arange(row_count, dtype=jnp.int32)) // block_size
    col_block = (col_first + jnp.arange(col_count, dtype=jnp.int32)) // block_size
    row_onehot = (row_block[:, None] == block_ids[None, :]).astype(jnp.float32)
    col_onehot = (col_block[:, None] == block_ids[None, :]).astype(jnp.float32)
    lookup = jnp.dot(jnp.dot(row_onehot, block_mask.astype(jnp.float32)), col_onehot.T)
    return jnp.logical_or(same_chain, lookup > 0.5)


def tri_gates(pair, gain_in, weights_in, allowed):
    channels = pair.shape[-1]
    normed = layer_norm(pair.astype(jnp.float32), gain_in).astype(jnp.bfloat16)
    projected = jnp.dot(normed, weights_in, preferred_element_type=jnp.float32)
    keep = allowed.astype(jnp.float32)[..., None]
    left_edge = (
        jax.nn.sigmoid(projected[..., :channels]) * projected[..., channels : 2 * channels] * keep
    ).astype(jnp.bfloat16)
    right_edge = (
        jax.nn.sigmoid(projected[..., 2 * channels : 3 * channels])
        * projected[..., 3 * channels : 4 * channels]
        * keep
    ).astype(jnp.bfloat16)
    gating = jax.nn.sigmoid(projected[..., 4 * channels :])
    return (left_edge, right_edge, gating)


def tri_finish(pair, combined, gain_out, weight_out, gating):
    normed = layer_norm(combined, gain_out).astype(jnp.bfloat16)
    update = gating * jnp.dot(normed, weight_out, preferred_element_type=jnp.float32)
    return (pair.astype(jnp.float32) + update).astype(jnp.bfloat16)


def per_device(
    pair,
    chain_id,
    block_mask,
    norm_gains,
    mult_in_weights,
    mult_out_weights,
    attn_weights,
    bias_weights,
    attn_out_weights,
):
    row_rows, col_cols, channels = pair.shape
    extent = row_rows * lax.axis_size("row")
    row_first = lax.axis_index("row") * row_rows
    col_first = lax.axis_index("col") * col_cols
    own_allowed = allowed_pairs(chain_id, block_mask, row_first, row_rows, col_first, col_cols, BLK)
    left_edge, right_edge, gating = tri_gates(pair, norm_gains[0], mult_in_weights[0], own_allowed)
    column_panel = lax.all_gather(right_edge, "row", axis=0, tiled=True)
    swapped = lax.psum_scatter(
        jnp.einsum(
            "jkc,ikc->jic", column_panel, left_edge, preferred_element_type=jnp.float32
        ).astype(jnp.bfloat16),
        "col",
        scatter_dimension=0,
        tiled=True,
    ).astype(jnp.float32)
    combined = jnp.transpose(swapped, (1, 0, 2))
    pair_one = tri_finish(pair, combined, norm_gains[1], mult_out_weights[0], gating)
    left_edge, right_edge, gating = tri_gates(
        pair_one, norm_gains[2], mult_in_weights[1], own_allowed
    )
    row_panel = lax.all_gather(left_edge, "col", axis=1, tiled=True)
    combined = lax.psum_scatter(
        jnp.einsum(
            "kic,kjc->ijc", row_panel, right_edge, preferred_element_type=jnp.float32
        ).astype(jnp.bfloat16),
        "row",
        scatter_dimension=0,
        tiled=True,
    ).astype(jnp.float32)
    pair_two = tri_finish(pair_one, combined, norm_gains[3], mult_out_weights[1], gating)
    head_count = bias_weights.shape[1]
    head_dim = channels // head_count
    normed = layer_norm(pair_two.astype(jnp.float32), norm_gains[4]).astype(jnp.bfloat16)
    projected = jnp.dot(normed, attn_weights, preferred_element_type=jnp.float32)
    queries = (projected[..., :channels] * head_dim ** (-0.5)).astype(jnp.bfloat16)
    gating = jax.nn.sigmoid(projected[..., 3 * channels :])
    own_keys = projected[..., channels : 2 * channels].astype(jnp.bfloat16)
    own_values = projected[..., 2 * channels : 3 * channels].astype(jnp.bfloat16)
    key_rows, value_rows = (
        lax.all_gather(own_keys, "col", axis=1, tiled=True),
        lax.all_gather(own_values, "col", axis=1, tiled=True),
    )
    pair_bias = jnp.dot(normed, bias_weights, preferred_element_type=jnp.float32).astype(
        jnp.bfloat16
    )
    bias_heads = jnp.transpose(pair_bias, (2, 0, 1))
    bias_panel = lax.all_gather(bias_heads, "col", axis=2, tiled=True)
    source_row = col_first // row_rows
    bias_source = from_root(bias_panel, "row", source_row)
    bias_query = lax.dynamic_slice_in_dim(
        bias_source, col_first - source_row * row_rows, col_cols, 1
    ).astype(jnp.float32)
    row_allowed = allowed_pairs(chain_id, block_mask, row_first, row_rows, 0, extent, BLK)
    penalty = jnp.where(row_allowed, 0.0, -1000000000.0).astype(jnp.float32)
    query_heads = queries.reshape(row_rows, col_cols, head_count, head_dim)
    key_heads = key_rows.reshape(row_rows, extent, head_count, head_dim)
    value_heads = value_rows.reshape(row_rows, extent, head_count, head_dim)
    rows_block = math.gcd(row_rows, 16)
    block_count = row_rows // rows_block

    def one_block(block_index):
        block_first = block_index * rows_block
        query_part = lax.dynamic_slice_in_dim(query_heads, block_first, rows_block, 0)
        key_part = lax.dynamic_slice_in_dim(key_heads, block_first, rows_block, 0)
        value_part = lax.dynamic_slice_in_dim(value_heads, block_first, rows_block, 0)
        penalty_part = lax.dynamic_slice_in_dim(penalty, block_first, rows_block, 0)
        scores = jnp.einsum(
            "ijhd,ikhd->ihjk", query_part, key_part, preferred_element_type=jnp.float32
        )
        scores = scores + bias_query[None] + penalty_part[:, None, None, :]
        raised = jnp.exp(scores)
        shares = (raised / jnp.sum(raised, axis=-1, keepdims=True)).astype(jnp.bfloat16)
        mixed = jnp.einsum(
            "ihjk,ikhd->ijhd", shares, value_part, preferred_element_type=jnp.float32
        ).reshape(rows_block, col_cols, channels)
        gating_part = lax.dynamic_slice_in_dim(gating, block_first, rows_block, 0)
        gated = (gating_part * mixed).astype(jnp.bfloat16)
        update = jnp.dot(gated, attn_out_weights, preferred_element_type=jnp.float32)
        residual_part = lax.dynamic_slice_in_dim(pair_two, block_first, rows_block, 0).astype(
            jnp.float32
        )
        return (residual_part + update).astype(jnp.bfloat16)

    blocks = lax.map(one_block, jnp.arange(block_count, dtype=jnp.int32))
    return blocks.reshape(row_rows, col_cols, channels)


def solution(mesh):
    placed = (P("row", "col", None), P(), P(), P(), P(), P(), P(), P(), P())
    return jax.shard_map(
        per_device, mesh=mesh, in_specs=placed, out_specs=P("row", "col", None), check_vma=False
    )
```

profile of v0, /device:TPU:1, one launch (start us, length us, event | category | flops | bytes accessed | tf_op | source)
XLA Modules:
  0.0 714.7 jit_solution(7769164381582863452)
XLA Ops:
  13.3 2.3 fusion.76
  15.6 2.3 copy-done.3
  21.0 54.2 %all-gather.5.cloned.1.call-done = bf16[512,32,128]{2,1,0:T(8,128)(2,1)} async-done(((bf16[64,32,128]{2,1,0:T(8,128)(2,1)}), bf16[512,32,128]{2,1,0:T(8,128)(2,1)}) %all-gather.5.cloned.1.call-update) | async-done | bytes 4194320 | tf_op jit(solution)/shard_map/all_gather | solution.py:76
  75.2 8.5 %copy.88 = bf16[512,32,128]{0,1,2:T(8,128)(2,1)} copy(bf16[512,32,128]{2,1,0:T(8,128)(2,1)} %all-gather.5.cloned.1.call-done) | data formatting | bytes 8388608 | tf_op jit(solution)/shard_map/all_gather | solution.py:76
  83.8 7.8 %convert_bitcast_fusion = bf16[512,64,128]{0,1,2:T(8,128)(2,1)} fusion(bf16[64,32,128]{0,1,2:T(8,128)(2,1)S(1)} %copy.87, bf16[512,32,128]{0,1,2:T(8,128)(2,1)} %copy.88), kind=kOutput, calls=%fused_computation.18 | convolution fusion | flops 272629760 | bytes 13107200 | tf_op jit(solution)/shard_map/jkc,ikc->jic/dot_general | solution.py:78
  91.6 13.7 %copy.89 = bf16[512,64,128]{2,1,0:T(8,128)(2,1)} copy(bf16[512,64,128]{0,1,2:T(8,128)(2,1)} %convert_bitcast_fusion) | data formatting | bytes 16777216 | tf_op jit(solution)/shard_map/convert_element_type | solution.py:80
  105.3 100.3 %reduce-scatter.3.cloned.1.call-done = bf16[32,64,128]{2,1,0:T(8,128)(2,1)} async-done(((bf16[512,64,128]{2,1,0:T(8,128)(2,1)}), bf16[32,64,128]{2,1,0:T(8,128)(2,1)}) %reduce-scatter.3.cloned.1.call-update) | async-done | bytes 524304 | tf_op jit(solution)/shard_map/reduce_scatter | solution.py:77
  214.3 2.4 copy-done.2
  220.1 75.7 %all-gather.7.cloned.1.call-done = bf16[64,512,128]{2,1,0:T(8,128)(2,1)} async-done(((bf16[64,32,128]{2,1,0:T(8,128)(2,1)}), bf16[64,512,128]{2,1,0:T(8,128)(2,1)}) %all-gather.7.cloned.1.call-update) | async-done | bytes 8388624 | tf_op jit(solution)/shard_map/all_gather | solution.py:90
  295.8 29.1 %copy.96 = bf16[64,512,128]{0,1,2:T(8,128)(2,1)} copy(bf16[64,512,128]{2,1,0:T(8,128)(2,1)} %all-gather.7.cloned.1.call-done) | data formatting | bytes 16777216 | tf_op jit(solution)/shard_map/all_gather | solution.py:90
  324.9 10.5 %convert_bitcast_fusion.1 = bf16[512,32,128]{0,1,2:T(8,128)(2,1)} fusion(bf16[64,32,128]{0,1,2:T(8,128)(2,1)S(1)} %copy.95, bf16[64,512,128]{0,1,2:T(8,128)(2,1)} %copy.96), kind=kOutput, calls=%fused_computation.19 | convolution fusion | flops 270532608 | bytes 13107200 | tf_op jit(solution)/shard_map/kic,kjc->ijc/dot_general | solution.py:92
  335.4 9.1 %copy.97 = bf16[512,32,128]{2,1,0:T(8,128)(2,1)} copy(bf16[512,32,128]{0,1,2:T(8,128)(2,1)} %convert_bitcast_fusion.1) | data formatting | bytes 8388608 | tf_op jit(solution)/shard_map/convert_element_type | solution.py:94
  344.6 50.2 %reduce-scatter.5.cloned.1.call-done = bf16[64,32,128]{2,1,0:T(8,128)(2,1)} async-done(((bf16[512,32,128]{2,1,0:T(8,128)(2,1)}), bf16[64,32,128]{2,1,0:T(8,128)(2,1)}) %reduce-scatter.5.cloned.1.call-update) | async-done | bytes 524304 | tf_op jit(solution)/shard_map/reduce_scatter | solution.py:91
  397.9 2.9 convert_reduce_fusion.2
  404.6 26.8 %all_gather.19 = bf16[4,64,512]{1,0,2:T(4,128)(2,1)S(1)} all-gather(bf16[4,64,32]{1,0,2:T(4,128)(2,1)S(1)} %copy.105), channel_id=1, replica_groups=mesh['row'=8,'col'=16] {'col'}, dimensions={2}, use_global_device_ids=true | all-gather | bytes 278528 | tf_op jit(solution)/shard_map/all_gather | solution.py:116
  432.5 3.7 fusion.112
  439.2 3.0 fusion.40
  442.8 3.2 copy.106
  446.1 49.9 %all-reduce.2.cloned.1.call-done = bf16[4,64,512]{1,0,2:T(4,128)(2,1)} async-done(((bf16[4,64,512]{1,0,2:T(4,128)(2,1)}), bf16[4,64,512]{1,0,2:T(4,128)(2,1)}) %all-reduce.2.cloned.1.call-update) | async-done | bytes 262160 | tf_op jit(solution)/shard_map/psum | solution.py:13
  498.4 82.3 %all-gather.9.cloned.1.call-done = bf16[64,512,128]{2,1,0:T(8,128)(2,1)} async-done(((bf16[64,32,128]{2,1,0:T(8,128)(2,1)}), bf16[64,512,128]{2,1,0:T(8,128)(2,1)}) %all-gather.9.cloned.1.call-update) | async-done | bytes 8388624 | tf_op jit(solution)/shard_map/all_gather | solution.py:110
  580.8 12.0 %copy.102 = bf16[64,512,128]{1,2,0:T(8,128)(2,1)} copy(bf16[64,512,128]{2,1,0:T(8,128)(2,1)} %all-gather.9.cloned.1.call-done) | data formatting | bytes 16777216 | tf_op jit(solution)/shard_map/all_gather | solution.py:110
  592.8 65.4 %all-gather.11.cloned.1.call-done = bf16[64,512,128]{2,1,0:T(8,128)(2,1)} async-done(((bf16[64,32,128]{2,1,0:T(8,128)(2,1)}), bf16[64,512,128]{2,1,0:T(8,128)(2,1)}) %all-gather.11.cloned.1.call-update) | async-done | bytes 8388624 | tf_op jit(solution)/shard_map/all_gather | solution.py:109
  658.1 11.9 %copy.104 = bf16[64,512,128]{1,2,0:T(8,128)(2,1)} copy(bf16[64,512,128]{2,1,0:T(8,128)(2,1)} %all-gather.11.cloned.1.call-done) | data formatting | bytes 16777216 | tf_op jit(solution)/shard_map/all_gather | solution.py:109
  670.0 36.9 %while.10 = (s32[]{:T(128)}, bf16[4,16,32,128]{3,2,1,0:T(8,128)(2,1)}, s32[4]{0:T(128)S(1)}, bf16[64,32,128]{2,1,0:T(8,128)(2,1)}, f32[64,32,128]{2,1,0:T(8,128)...) while((s32[]{:T(128)}, ...), condition=%wide.region_15.16_spmd, body=%wide.region_13.15_spmd.sunk | while | flops 158660608 | bytes 15387343 | solution.py:153
  672.1 2.5 fusion.126
  674.7 2.4 fusion.127
  681.4 2.5 fusion.126
  683.9 2.4 fusion.127
  690.6 2.5 fusion.126
  693.1 2.4 fusion.127
  699.8 2.5 fusion.126
  702.3 2.4 fusion.127
  (96 shorter events, 50.9 us)
Async XLA Ops:
  6.5 425.9 %copy-start = (bf16[128,512]{1,0:T(8,128)(2,1)S(1)}, bf16[128,512]{1,0:T(8,128)(2,1)}, u32[]{:S(2)}) copy-start(bf16[128,512]{1,0:T(8,128)(2,1)} %param.17) | copy-start | bytes 393220
  6.5 68.7 %all-gather.5.cloned.1.call-start = ((), (), s32[]{:S(2)}) async-start(), calls=%async_computation.2 | async-start | bytes 4718592 | tf_op jit(solution)/shard_map/all_gather | solution.py:76
  15.5 2.3 copy-start.3
  19.3 186.3 %reduce-scatter.3.cloned.1.call-start = ((), (), s32[]{:S(2)}) async-start(), calls=%async_computation.3 | async-start | bytes 8912896 | tf_op jit(solution)/shard_map/reduce_scatter | solution.py:77
  105.2 105.5 %copy-start.4 = (bf16[64,32,128]{2,1,0:T(8,128)(2,1)S(1)}, bf16[64,32,128]{2,1,0:T(8,128)(2,1)}, u32[]{:S(2)}) copy-start(bf16[64,32,128]{2,1,0:T(8,128)(2,1)} %param.11) | copy-start | bytes 1572868
  105.2 105.5 %copy-start.7 = (bf16[2,128,128]{2,1,0:T(8,128)(2,1)S(1)}, bf16[2,128,128]{2,1,0:T(8,128)(2,1)}, u32[]{:S(2)}) copy-start(bf16[2,128,128]{2,1,0:T(8,128)(2,1)} %param.16) | copy-start | bytes 196612
  105.3 190.5 %all-gather.7.cloned.1.call-start = ((), (), s32[]{:S(2)}) async-start(), calls=%async_computation.4 | async-start | bytes 8912896 | tf_op jit(solution)/shard_map/all_gather | solution.py:90
  208.8 4.5 copy-start.6
  214.3 2.4 copy-start.2
  218.1 176.7 %reduce-scatter.5.cloned.1.call-start = ((), (), s32[]{:S(2)}) async-start(), calls=%async_computation.5 | async-start | bytes 4718592 | tf_op jit(solution)/shard_map/reduce_scatter | solution.py:91
  344.5 151.5 %all-reduce.2.cloned.1.call-start = ((), (), s32[]{:S(2)}) async-start(), calls=%async_computation.8 | async-start | bytes 1048576 | tf_op jit(solution)/shard_map/psum | solution.py:13
  396.2 6.3 copy-start.9
  432.4 5.8 copy-start.8
  432.4 148.4 %all-gather.9.cloned.1.call-start = ((), (), s32[]{:S(2)}) async-start(), calls=%async_computation.6 | async-start | bytes 8912896 | tf_op jit(solution)/shard_map/all_gather | solution.py:110
  437.4 220.7 %all-gather.11.cloned.1.call-start = ((), (), s32[]{:S(2)}) async-start(), calls=%async_computation.7 | async-start | bytes 8912896 | tf_op jit(solution)/shard_map/all_gather | solution.py:109
  592.8 77.2 %copy-start.5 = (bf16[128,128]{1,0:T(8,128)(2,1)S(1)}, bf16[128,128]{1,0:T(8,128)(2,1)}, u32[]{:S(2)}) copy-start(bf16[128,128]{1,0:T(8,128)(2,1)} %param.19) | copy-start | bytes 98308
  706.9 0.9 copy-start.1
Sparse Core Ops, SparseCore 0:
  19.4 55.7 all-gather.4
  105.4 100.1 reduce-scatter.2
  218.2 77.4 all-gather.6
  344.6 50.1 reduce-scatter.4
  432.5 63.4 all-reduce.1
  498.5 82.2 all-gather.8
  583.4 74.6 all-gather.10
where the time goes:
time: 717 us; the launch traced here: 715 us
  waiting for transfers between devices  479 us (67%)
  local copies, waits for them, and re-layouts  109 us (15%)
  matrix products  61.1 us (9%)
  blocking collectives  26.8 us (4%)
  other arithmetic  21.4 us (3%)
  between operations  13.8 us (2%)
    reduce_scatter x1, waiting for transfers between devices, per_device(): lax.psum_scatter(jnp.einsum('jkc,ikc->jic', column_panel, left_edge, pref...  100 us
    all_gather x1, waiting for transfers between devices, per_device(): lax.all_gather(own_values, 'col', axis=1, tiled=True)  82.3 us
    all_gather x1, waiting for transfers between devices, per_device(): row_panel = lax.all_gather(left_edge, 'col', axis=1, tiled=True)  75.7 us
    all_gather x1, waiting for transfers between devices, per_device(): lax.all_gather(own_keys, 'col', axis=1, tiled=True)  65.4 us
    all_gather x1, waiting for transfers between devices, per_device(): column_panel = lax.all_gather(right_edge, 'row', axis=0, tiled=True)  54.2 us
    reduce_scatter x1, waiting for transfers between devices, per_device(): lax.psum_scatter(jnp.einsum('kic,kjc->ijc', row_panel, right_edge, prefer...  50.2 us
    psum x1, waiting for transfers between devices, from_root(): return lax.psum(kept, axis)  49.9 us
    all_gather x1, local copies, waits for them, and re-layouts, per_device(): row_panel = lax.all_gather(left_edge, 'col', axis=1, tiled=True)  29.1 us
  transfers between devices with their start and end apart: 7, of which 7 were waited for; matrix products, arithmetic and copies ran while one was open for 4% of the time, Pallas kernels for 0%

commit v1 on v0

v1 whole, which is shorter than its diff:
```python
import functools

import jax
import jax.numpy as jnp
from jax import lax
from jax.experimental import pallas as pl
from jax.experimental.pallas import tpu as pltpu
from jax.sharding import PartitionSpec as P

MESH = pl.DeviceIdType.MESH
F32 = jnp.float32
BF16 = jnp.bfloat16
ROWS = 8
COLS = 16
DEV = ROWS * COLS
C = 128
N = 512
H = 4
OWN = 4


def dot(a, b):
    return jnp.dot(a, b, preferred_element_type=F32)


def dot_nt(a, b):
    return lax.dot_general(a, b, (((1,), (1,)), ((), ())), preferred_element_type=F32)


def norm_cm(x, gain):
    center = x - jnp.mean(x, axis=0, keepdims=True)
    spread = jnp.mean(center * center, axis=0, keepdims=True)
    return center * lax.rsqrt(spread + 1e-05) * gain


def kernel(
    pair,
    chain_s,
    chain_v,
    block_s,
    gains,
    w_in,
    w_out,
    w_attn,
    w_bias,
    w_final,
    out,
    rows_in,
    pair_cm,
    gate_cm,
    norm_c,
    keep,
    gain_b,
    wt_in,
    wt_out,
    wt_k,
    wt_bias,
    wide,
    edges,
    send_a,
    recv_a,
    send_b,
    recv_b,
    bias_send,
    bias_recv,
    bias_wide,
    bias_nat,
    q_ext,
    k_ext,
    v_ext,
    rows_out,
    sem_send,
    sem_recv,
):
    r = lax.axis_index("row")
    c = lax.axis_index("col")
    me = r * COLS + c

    def device(t):
        return (lax.div(t, COLS), lax.rem(t, COLS))

    barrier = pltpu.get_barrier_semaphore()

    @pl.loop(1, DEV)
    def _(step):
        pl.semaphore_signal(
            barrier, inc=1, device_id=device(lax.rem(me + step, DEV)), device_id_type=MESH
        )

    for n in range(5):
        gain_b[n] = jnp.transpose(jnp.broadcast_to(gains[n : n + 1, :], (C, C)))
    for t in range(2):
        for g in range(5):
            part = w_in[t, :, g * C : (g + 1) * C].astype(F32)
            wt_in[t, g * C : (g + 1) * C, :] = jnp.transpose(part).astype(BF16)
        wt_out[t] = jnp.transpose(w_out[t].astype(F32)).astype(BF16)
    wt_k[...] = jnp.transpose(w_attn[:, C : 2 * C].astype(F32)).astype(BF16)
    wt_bias[...] = jnp.transpose(w_bias[...].astype(F32)).astype(BF16)
    block_of = lax.broadcasted_iota(jnp.int32, (1, N), 1) // 64
    linked = jnp.zeros((1, N), jnp.int32)
    for nb in range(8):
        linked = jnp.where(block_of == nb, block_s[r, nb], linked)
    for a in range(OWN):
        own_chain = chain_s[r * 64 + a * 16 + c]
        allowed = jnp.logical_or(chain_v[...] == own_chain, linked == 1)
        keep[a : a + 1, :] = jnp.where(allowed, 1.0, 0.0).astype(F32)

    pl.semaphore_wait(barrier, DEV - 1)

    pltpu.make_async_copy(
        pair.at[:, c], rows_in.at[:, pl.ds(c * 32, 32)], sem_recv.at[0]
    ).start()

    @pl.loop(1, COLS)
    def _(step):
        t = lax.rem(c + step, COLS)
        pltpu.make_async_remote_copy(
            pair.at[:, t],
            rows_in.at[:, pl.ds(c * 32, 32)],
            sem_send.at[0],
            sem_recv.at[0],
            device_id=(r, t),
            device_id_type=MESH,
        ).start()

    pltpu.make_async_copy(rows_in, rows_in, sem_recv.at[0]).wait()

    @pl.loop(0, OWN)
    def _(a):
        x = jnp.transpose(rows_in[a].astype(F32))
        pair_cm[a] = x
        norm_c[a] = norm_cm(x, jnp.tile(gain_b[0], (1, 4))).astype(BF16)

    def send_chunk(source, target, t, k):
        @pl.when(t == me)
        def _():
            pltpu.make_async_copy(source.at[t], target.at[me], sem_recv.at[k]).start()

        @pl.when(t != me)
        def _():
            pltpu.make_async_remote_copy(
                source.at[t],
                target.at[me],
                sem_send.at[k],
                sem_recv.at[k],
                device_id=device(t),
                device_id_type=MESH,
            ).start()

    def send_edges(t, k):
        @pl.loop(0, 4)
        def _(step):
            base = pl.multiple_of(lax.rem(lax.div(me, 32) + step, 4) * 32, 32)
            for a in range(OWN):
                x = norm_c[a]
                mask = keep[a : a + 1, :]
                for side in range(2):
                    g = dot(wt_in[t, pl.ds(2 * side * C + base, 32), :], x)
                    v = dot(wt_in[t, pl.ds((2 * side + 1) * C + base, 32), :], x)
                    e = jax.nn.sigmoid(g) * v * mask
                    for b in range(4):
                        wide[pl.ds(base * 32 + side * 16 + a * 4 + b, 32, stride=32), :] = e[
                            :, b * 128 : (b + 1) * 128
                        ]
            part = wide[pl.ds(pl.multiple_of(base * 32, 1024), 1024), :]
            send_a[t, pl.ds(base, 32)] = part.reshape(32, 32, 128).astype(BF16)

            @pl.loop(0, 32)
            def _(s):
                send_chunk(send_a.at[t], recv_a.at[t], base + lax.rem(me + s, 32), k)

        for a in range(OWN):
            gate_cm[a] = jax.nn.sigmoid(dot(wt_in[t, 4 * C : 5 * C, :], norm_c[a]))

    def triangle(t, k):
        pltpu.make_async_copy(recv_a.at[t], recv_a.at[t], sem_recv.at[k]).wait()

        @pl.loop(0, ROWS)
        def _(q):
            first = pl.multiple_of(q * 512, 512)
            wide[pl.ds(first, 512), :] = (
                recv_a[t, pl.ds(q * 16, 16)].astype(F32).reshape(512, 128)
            )
            for side in range(2):
                for a in range(OWN):
                    for b in range(4):
                        block = wide[pl.ds(first + side * 16 + a * 4 + b, 16, stride=32), :]
                        edges[
                            side, pl.ds(q * 64 + a * 16, 16), b * 128 : (b + 1) * 128
                        ] = block.astype(BF16)

        @pl.loop(0, 4)
        def _(step):
            q = lax.rem(lax.div(me, 32) + step, 4)
            if t == 0:
                left = edges[0, pl.ds(pl.multiple_of(q * 128, 128), 128), :]
                total = dot_nt(left, edges[1])
            else:
                left = edges[0, :, pl.ds(pl.multiple_of(q * 128, 128), 128)]
                total = dot(jnp.transpose(left.astype(F32)).astype(BF16), edges[1])
            for half in range(2):
                for a in range(OWN):
                    for b in range(4):
                        wide[
                            pl.ds(q * 512 + half * 256 + a * 4 + b, 16, stride=16), :
                        ] = total[
                            half * 64 + a * 16 : half * 64 + a * 16 + 16,
                            b * 128 : (b + 1) * 128,
                        ]
            part = wide[pl.ds(pl.multiple_of(q * 512, 512), 512), :]
            send_b[t, pl.ds(q * 32, 32)] = part.reshape(32, 16, 128).astype(BF16)

            @pl.loop(0, 32)
            def _(s):
                send_chunk(send_b.at[t], recv_b.at[t], q * 32 + lax.rem(me + s, 32), k + 1)

    def finish(t, k, then):
        pltpu.make_async_copy(recv_b.at[t], recv_b.at[t], sem_recv.at[k]).wait()
        wide[0:2048, :] = recv_b[t].astype(F32).reshape(2048, 128)

        @pl.loop(0, OWN)
        def _(a):
            total = jnp.concatenate(
                [wide[pl.ds(a * 4 + b, 128, stride=16), :] for b in range(4)], axis=1
            )
            normed = norm_cm(total, jnp.tile(gain_b[2 * t + 1], (1, 4))).astype(BF16)
            update = gate_cm[a] * dot(wt_out[t], normed)
            new = (pair_cm[a] + update).astype(BF16).astype(F32)
            pair_cm[a] = new
            then(a, norm_cm(new, jnp.tile(gain_b[2 * t + 2], (1, 4))))

    send_edges(0, 1)
    triangle(0, 1)

    def keep_norm(a, normed):
        norm_c[a] = normed.astype(BF16)

    finish(0, 2, keep_norm)
    send_edges(1, 3)
    triangle(1, 3)

    def bias_part(a, normed):
        rounded = normed.astype(BF16)
        norm_c[a] = rounded
        bias = dot(wt_bias[...], rounded)
        for kb in range(4):
            bias_wide[pl.ds(kb * 16 + a, 4, stride=4), :] = bias[
                0:H, kb * 128 : (kb + 1) * 128
            ]

    finish(1, 4, bias_part)
    bias_send[...] = bias_wide[0:64, :].reshape(4, 16, 128).astype(BF16)

    pltpu.make_async_copy(bias_send, bias_recv.at[me], sem_recv.at[5]).start()

    @pl.loop(1, DEV)
    def _(step):
        pltpu.make_async_remote_copy(
            bias_send,
            bias_recv.at[me],
            sem_send.at[5],
            sem_recv.at[5],
            device_id=device(lax.rem(me + step, DEV)),
            device_id_type=MESH,
        ).start()

    lane = lax.broadcasted_iota(jnp.int32, (N, C), 1)
    first_row = lax.broadcasted_iota(jnp.int32, (C, N), 0) == 0
    q_ext[:, :, C:] = jnp.where(lane == 0, 1.0, 0.0).astype(BF16)[None] * jnp.ones(
        (OWN, 1, 1), BF16
    )
    v_ext[:, C:] = jnp.ones((N, C), BF16)

    @pl.loop(0, OWN)
    def _(a):
        k_ext[a, 0:C, :] = dot(wt_k[...], norm_c[a]).astype(BF16)
        penalty = jnp.where(keep[pl.ds(a, 1), :] > 0.5, 0.0, -1e9)
        k_ext[a, C:, :] = jnp.where(first_row, penalty, 0.0).astype(BF16)
        rows = jnp.transpose(norm_c[a].astype(F32)).astype(BF16)
        rows_in[a] = rows
        q_ext[a, :, 0:C] = (dot(rows, w_attn[:, 0:C]) * 32**-0.5).astype(BF16)

    pltpu.make_async_copy(bias_recv, bias_recv, sem_recv.at[5]).wait()

    @pl.loop(0, ROWS)
    def _(q):
        bias_wide[...] = bias_recv[pl.ds(q * 16, 16)].astype(F32).reshape(1024, 128)
        for h in range(H):
            for a in range(OWN):
                for kb in range(4):
                    bias_nat[
                        h, pl.ds(q * 64 + a * 16, 16), kb * 128 : (kb + 1) * 128
                    ] = bias_wide[pl.ds(kb * 16 + h * 4 + a, 16, stride=64), :]

    @pl.loop(0, OWN)
    def _(a):
        rows = rows_in[a]
        values = dot(rows, w_attn[:, 2 * C : 3 * C])
        total = jnp.zeros((N, C), F32)
        for h in range(H):
            here = jnp.logical_and(lane >= 32 * h, lane < 32 * (h + 1))
            v_ext[:, 0:C] = jnp.where(here, values, 0.0).astype(BF16)
            lane2 = lax.broadcasted_iota(jnp.int32, (N, 2 * C), 1)
            here2 = jnp.logical_or(
                jnp.logical_and(lane2 >= 32 * h, lane2 < 32 * (h + 1)), lane2 >= C
            )
            query = jnp.where(here2, q_ext[a].astype(F32), 0.0).astype(BF16)
            scores = dot(query, k_ext[a]) + bias_nat[h]
            raised = jnp.exp(scores).astype(BF16)
            mixed = dot(raised, v_ext[...])
            total = total + mixed[:, 0:C] / mixed[:, C:]
        gating = jax.nn.sigmoid(dot(rows, w_attn[:, 3 * C :]))
        gated = (gating * total).astype(BF16)
        update = dot(gated, w_final[...])
        rows_out[a] = (jnp.transpose(pair_cm[a]) + update).astype(BF16)

    pltpu.make_async_copy(
        rows_out.at[:, pl.ds(c * 32, 32)], out.at[:, c], sem_recv.at[6]
    ).start()

    @pl.loop(1, COLS)
    def _(step):
        t = lax.rem(c + step, COLS)
        pltpu.make_async_remote_copy(
            rows_out.at[:, pl.ds(t * 32, 32)],
            out.at[:, c],
            sem_send.at[6],
            sem_recv.at[6],
            device_id=(r, t),
            device_id_type=MESH,
        ).start()

    pltpu.make_async_copy(out, out, sem_recv.at[6]).wait()

    def sent(array, k):
        pltpu.make_async_copy(array, array, sem_send.at[k]).wait()

    sent(out.at[:, pl.ds(0, COLS - 1)], 0)
    sent(out.at[:, pl.ds(0, COLS - 1)], 6)
    for t in range(2):
        sent(recv_a.at[t, pl.ds(0, DEV - 1)], 2 * t + 1)
        sent(recv_b.at[t, pl.ds(0, DEV - 1)], 2 * t + 2)
    sent(bias_recv.at[pl.ds(0, DEV - 1)], 5)


def per_device(
    pair, chain_id, block_mask, norm_gains, w_in, w_out, w_attn, w_bias, w_final
):
    vmem = pl.BlockSpec(memory_space=pltpu.VMEM)
    smem = pl.BlockSpec(memory_space=pltpu.SMEM)
    result = pl.pallas_call(
        kernel,
        out_shape=jax.ShapeDtypeStruct((OWN, COLS, 32, C), BF16),
        in_specs=[vmem, smem, vmem, smem] + [vmem] * 6,
        out_specs=vmem,
        scratch_shapes=[
            pltpu.VMEM((OWN, N, C), BF16),
            pltpu.VMEM((OWN, C, N), F32),
            pltpu.VMEM((OWN, C, N), F32),
            pltpu.VMEM((OWN, C, N), BF16),
            pltpu.VMEM((8, N), F32),
            pltpu.VMEM((5, C, C), F32),
            pltpu.VMEM((2, 5 * C, C), BF16),
            pltpu.VMEM((2, C, C), BF16),
            pltpu.VMEM((C, C), BF16),
            pltpu.VMEM((16, C), BF16),
            pltpu.VMEM((4096, C), F32),
            pltpu.VMEM((2, N, N), BF16),
            pltpu.VMEM((2, DEV, 32, C), BF16),
            pltpu.VMEM((2, DEV, 32, C), BF16),
            pltpu.VMEM((2, DEV, 16, C), BF16),
            pltpu.VMEM((2, DEV, 16, C), BF16),
            pltpu.VMEM((4, 16, C), BF16),
            pltpu.VMEM((DEV, 4, 16, C), BF16),
            pltpu.VMEM((1024, C), F32),
            pltpu.VMEM((H, N, N), F32),
            pltpu.VMEM((OWN, N, 2 * C), BF16),
            pltpu.VMEM((OWN, 2 * C, N), BF16),
            pltpu.VMEM((N, 2 * C), BF16),
            pltpu.VMEM((OWN, N, C), BF16),
            pltpu.SemaphoreType.DMA((7,)),
            pltpu.SemaphoreType.DMA((7,)),
        ],
        name="triangle_block",
        compiler_params=pltpu.CompilerParams(
            collective_id=0, has_side_effects=True, vmem_limit_bytes=56 << 20
        ),
        cost_estimate=pl.CostEstimate(
            flops=3 * 10**9, bytes_accessed=2 * 10**6, transcendentals=5 * 10**6
        ),
    )(
        pair.reshape(OWN, COLS, 32, C),
        chain_id,
        chain_id.reshape(1, N),
        block_mask,
        norm_gains,
        w_in,
        w_out,
        w_attn,
        jnp.pad(w_bias, ((0, 0), (0, 12))),
        w_final,
    )
    return result.reshape(64, 32, C)


def solution(mesh):
    placed = (P("row", "col", None), P(), P(), P(), P(), P(), P(), P(), P())
    return jax.shard_map(
        per_device, mesh=mesh, in_specs=placed, out_specs=P("row", "col", None), check_vma=False
    )
```

time: 717 us -> 145 us (0.20)
  waiting for transfers between devices: 479 us -> 0 us
  Pallas kernels: 0 us -> 141 us
  local copies, waits for them, and re-layouts: 109 us -> 3.31 us
  matrix products: 61.1 us -> 0 us
  blocking collectives: 26.8 us -> 0 us
  other arithmetic: 21.4 us -> 0 us
  between operations: 13.8 us -> 0.01 us
    all_gather x4 -> x0, waiting for transfers between devices: 278 us -> none  [the longest x1 82.3 us: per_device(): lax.all_gather(own_values, 'col', axis=1, tiled=True)]
    reduce_scatter x2 -> x0, waiting for transfers between devices: 151 us -> none  [the longest x1 100 us: per_device(): lax.psum_scatter(jnp.einsum('jkc,ikc->jic', column_panel, left_edge, pref...]
    pallas_call x0 -> x1, Pallas kernels: none -> 141 us  [per_device(): pl.pallas_call(kernel, out_shape=jax.ShapeDtypeStruct((OWN, COLS, 32, C),...]
    all_gather x4 -> x0, local copies, waits for them, and re-layouts: 61.6 us -> none  [the longest x1 29.1 us: per_device(): row_panel = lax.all_gather(left_edge, 'col', axis=1, tiled=True)]
    dot_general x23 -> x0, matrix products: 61.1 us -> none  [the longest x1 10.5 us: per_device(): jnp.einsum('kic,kjc->ijc', row_panel, right_edge, preferred_element_type=...]
    psum x1 -> x0, waiting for transfers between devices: 49.9 us -> none  [from_root(): return lax.psum(kept, axis)]
    convert_element_type x7 -> x0, local copies, waits for them, and re-layouts: 27.1 us -> none  [the longest x1 13.7 us: per_device(): swapped = lax.psum_scatter(jnp.einsum('jkc,ikc->jic', column_panel, left_...]
    all_gather x1 -> x0, blocking collectives: 26.8 us -> none  [per_device(): bias_panel = lax.all_gather(bias_heads, 'col', axis=2, tiled=True)]
  transfers between devices with their start and end apart: 7 -> 0, of which waited for: 7 -> 0; matrix products, arithmetic and copies ran while one was open for 4% -> 0% of each run, Pallas kernels for 0% -> 0%
where the time goes in v1:
time: 145 us
  Pallas kernels  141 us (97%)
  local copies, waits for them, and re-layouts  3.31 us (2%)
    pallas_call x1, Pallas kernels, per_device(): pl.pallas_call(kernel, out_shape=jax.ShapeDtypeStruct((OWN, COLS, 32, C),...  141 us

profile of v1, /device:TPU:1, one launch (start us, length us, event | category | flops | bytes accessed | tf_op | source)
XLA Modules:
  0.0 144.6 jit_solution(11025421798483747941)
XLA Ops:
  0.0 0.0 copy-start
  0.0 0.7 copy-done
  0.7 0.1 copy.10
  0.8 0.6 pad.4.w_bias
  1.4 141.3 %triangle_block.1 = bf16[4,16,32,128]{3,2,1,0:T(8,128)(2,1)} custom-call(bf16[4,16,32,128]{3,2,1,0:T(8,128)(2,1)} %bitcast.4, s32[512]{0:T(512)} %chain_s.1, s32[1,512]{1,0:T(1,128)} %bitcast.5, s32[8,8]{1,0:T(8,128)} %block_s.1, f32[5,128]{1,0:T(8,128)} %gains.1, bf16[2,128,640]{2,1,0:T(8,128)(2,1)} %w_in.1, bf16[2,128,128]{2,1,0:T(8,128)(2,1)} %w_out.1, ...), custom_call_target="tpu_custom_call" | custom-call | flops 3000000000 | bytes 2000000 | tf_op jit(solution)/shard_map/triangle_block/pallas_call | solution.py:351
  142.7 1.9 %copy.12 = bf16[64,32,128]{2,1,0:T(8,128)(2,1)} copy(bf16[64,32,128]{2,1,0:T(8,128)(2,1)} %bitcast.3) | data formatting | bytes 1048576
Async XLA Ops:
  0.0 0.7 copy-start

commit v2 on v1

v2 whole, which is shorter than its diff:
```python
import jax
import jax.numpy as jnp
from jax import lax
from jax.experimental import pallas as pl
from jax.experimental.pallas import tpu as pltpu
from jax.sharding import PartitionSpec as P

MESH = pl.DeviceIdType.MESH
F32 = jnp.float32
BF16 = jnp.bfloat16
ROWS = 8
COLS = 16
DEV = ROWS * COLS
CHIPS = DEV // 2
C = 128
N = 512
HALF = N // 2
H = 4
OWN = 4
LOG2E = 1.4426950408889634

FAR = (
    (699248298, 5),
    (791255470, 5),
    (966748069, 5),
    (770581915, 5),
    (199256638, 5),
    (744454258, 5),
    (160421045, 5),
    (612196317, 5),
    (322204568, 5),
    (336278469, 5),
    (539184252, 5),
    (51578641, 5),
    (49232, 3),
)


def dot(a, b):
    return jnp.dot(a, b, preferred_element_type=F32)


def norm_cm(x, gain):
    center = x - jnp.mean(x, axis=0, keepdims=True)
    spread = jnp.mean(center * center, axis=0, keepdims=True)
    return center * lax.rsqrt(spread + 1e-05) * gain


def kernel(
    pair,
    chain_s,
    chain_v,
    block_s,
    gains,
    w_in,
    w_out,
    w_attn,
    w_bias,
    w_final,
    out,
    rows_in,
    pair_cm,
    gate_cm,
    norm8,
    norm_0,
    keep8,
    keep_0,
    gain_b,
    wt_in,
    wt_out,
    wt_k,
    wide,
    edges,
    send_a,
    recv_a,
    send_b,
    recv_b,
    bias_send,
    bias_recv,
    bias_nat,
    half_send,
    resid8,
    q_ext,
    k_ext,
    v_ext,
    gate8,
    total8,
    rows_out,
    sem_send,
    sem_recv,
):
    r = lax.axis_index("row")
    c = lax.axis_index("col")
    core = lax.rem(c, 2)
    duo = lax.div(c, 2)
    chip = r * 8 + duo
    me = core * CHIPS + chip
    place = core * 8 + duo
    other = 1 - core
    cx = lax.rem(duo, 2) * 2 + lax.div(r, 4)
    cy = lax.rem(r, 4)
    cz = lax.div(duo, 2)

    barrier = pltpu.get_barrier_semaphore()

    @pl.loop(1, DEV)
    def _(step):
        t = lax.rem(r * COLS + c + step, DEV)
        pl.semaphore_signal(
            barrier, inc=1, device_id=(lax.div(t, COLS), lax.rem(t, COLS)), device_id_type=MESH
        )

    def far_chips(visit):
        for packed, count in FAR:

            def body(_, value):
                d = lax.rem(value, 64)
                x = lax.rem(cx + lax.rem(d, 4), 4)
                y = lax.rem(cy + lax.rem(lax.div(d, 4), 4), 4)
                z = lax.rem(cz + lax.div(d, 16), 4)
                visit(lax.rem(x, 2) * 4 + y, z * 2 + lax.div(x, 2))
                return lax.div(value, 64)

            lax.fori_loop(0, count, body, jnp.int32(packed))

    def chunk(source, target, k, r2, duo2, core2):
        t = core2 * CHIPS + r2 * 8 + duo2
        pltpu.make_async_remote_copy(
            source.at[t],
            target.at[me],
            sem_send.at[k],
            sem_recv.at[k],
            device_id=(r2, duo2 * 2 + core2),
            device_id_type=MESH,
        ).start()

    def send_far(source, target, k, cores):
        def visit(r2, duo2):
            for core2 in cores:
                chunk(source, target, k, r2, duo2, core2)

        far_chips(visit)

    def send_near(source, target, k):
        pltpu.make_async_copy(source.at[me], target.at[me], sem_recv.at[k]).start()
        chunk(source, target, k, r, duo, other)

    def arrived(array, k):
        pltpu.make_async_copy(array, array, sem_recv.at[k]).wait()

    def sent(array, k):
        pltpu.make_async_copy(array, array, sem_send.at[k]).wait()

    def make_edges(t, base, normed, mask):
        for a in range(OWN):
            x = normed[a]
            m = mask[a : a + 1, :]
            for side in range(2):
                g = dot(wt_in[t, pl.ds(2 * side * C + base, 32), :], x)
                v = dot(wt_in[t, pl.ds((2 * side + 1) * C + base, 32), :], x)
                e = jax.nn.sigmoid(g) * v * m
                for b in range(4):
                    wide[pl.ds(base * 32 + side * 16 + a * 4 + b, 32, stride=32), :] = e[
                        :, b * 128 : (b + 1) * 128
                    ]
        part = wide[pl.ds(pl.multiple_of(base * 32, 1024), 1024), :]
        send_a[t, pl.ds(base, 32)] = part.reshape(32, 32, 128).astype(BF16)

    for n in range(5):
        gain_b[n] = jnp.transpose(jnp.broadcast_to(gains[n : n + 1, :], (C, C)))
    for t in range(2):
        for g in range(5):
            part = w_in[t, :, g * C : (g + 1) * C].astype(F32)
            wt_in[t, g * C : (g + 1) * C, :] = jnp.transpose(part).astype(BF16)
        wt_out[t] = jnp.transpose(w_out[t].astype(F32)).astype(BF16)
    wt_k[...] = jnp.transpose(w_attn[:, C : 2 * C].astype(F32)).astype(BF16)

    block_of = lax.broadcasted_iota(jnp.int32, (1, N), 1) // 64
    linked = jnp.zeros((1, N), jnp.int32)
    for nb in range(8):
        linked = jnp.where(block_of == nb, block_s[r, nb], linked)
    for i in range(2 * OWN):
        at = place if i < OWN else other * 8 + duo
        own_chain = chain_s[r * 64 + (i % OWN) * 16 + at]
        allowed = jnp.logical_or(chain_v[...] == own_chain, linked == 1)
        keep8[i : i + 1, :] = jnp.where(allowed, 1.0, 0.0).astype(F32)

    lane = lax.broadcasted_iota(jnp.int32, (1, C), 1)
    row_of = lax.rem(lane, 64)

    def pick(il, chains):
        return jnp.where(row_of == il, chain_s[r * 64 + il], chains)

    row_chain = lax.fori_loop(0, 64, pick, jnp.zeros((1, C), jnp.int32))
    block_on = block_s[r, duo]
    for s in range(16):
        col_chain = jnp.where(lane < 64, chain_s[c * 32 + s], chain_s[c * 32 + 16 + s])
        allowed = jnp.logical_or(row_chain == col_chain, block_on == 1)
        keep_0[s // 4 : s // 4 + 1, (s % 4) * 128 : (s % 4 + 1) * 128] = jnp.where(
            allowed, 1.0, 0.0
        ).astype(F32)

    wide[0:2048, :] = pair[...].astype(F32).reshape(2048, C)

    @pl.loop(0, 4)
    def _(a):
        for b in range(4):
            s = a * 4 + b
            x = jnp.concatenate(
                [wide[pl.ds(s, 64, stride=32), :], wide[pl.ds(16 + s, 64, stride=32), :]], axis=0
            )
            norm_0[a, :, b * 128 : (b + 1) * 128] = norm_cm(jnp.transpose(x), gain_b[0]).astype(
                BF16
            )

    @pl.loop(0, 4)
    def _(step):
        make_edges(0, pl.multiple_of(step * 32, 32), norm_0, keep_0)

    pl.semaphore_wait(barrier, DEV - 1)

    send_far(send_a.at[0], recv_a.at[0], 1, (0, 1))
    send_near(send_a.at[0], recv_a.at[0], 1)

    pltpu.make_async_copy(
        pair.at[:, place], rows_in.at[:, pl.ds(c * 32, 32)], sem_recv.at[0]
    ).start()

    @pl.loop(1, COLS)
    def _(step):
        t = lax.rem(c + step, COLS)
        pltpu.make_async_remote_copy(
            pair.at[:, lax.rem(t, 2) * 8 + lax.div(t, 2)],
            rows_in.at[:, pl.ds(c * 32, 32)],
            sem_send.at[0],
            sem_recv.at[0],
            device_id=(r, t),
            device_id_type=MESH,
        ).start()

    def triangle(t, k):
        arrived(recv_a.at[t], k)
        if t == 0:
            low = lax.broadcasted_iota(jnp.int32, (C, C), 1) < 64
            for side in range(2):
                for q in range(4):

                    @pl.loop(0, 2)
                    def _(k2):
                        first = k2 * CHIPS + 2 * q * 8
                        here = recv_a[t, pl.ds(first, 8), side * 16 : side * 16 + 16]
                        there = recv_a[t, pl.ds(first + 8, 8), side * 16 : side * 16 + 16]
                        here = here.astype(F32).reshape(C, C)
                        there = there.astype(F32).reshape(C, C)
                        at = pl.multiple_of(k2 * 128, 128)
                        edges[side, pl.ds(at, 128), q * 128 : (q + 1) * 128] = jnp.where(
                            low, here, pltpu.roll(there, 64, 1)
                        ).astype(BF16)
                        edges[side, pl.ds(at + 256, 128), q * 128 : (q + 1) * 128] = jnp.where(
                            low, pltpu.roll(here, 64, 1), there
                        ).astype(BF16)
        else:
            wide[...] = recv_a[t].astype(F32).reshape(4096, 128)
            for side in range(2):
                for b in range(4):

                    @pl.loop(0, OWN)
                    def _(a):
                        block = wide[pl.ds(side * 16 + a * 4 + b, 128, stride=32), :]
                        edges[
                            side, pl.ds(pl.multiple_of(a * 128, 128), 128), b * 128 : (b + 1) * 128
                        ] = block.astype(BF16)

        @pl.loop(0, 4)
        def _(q):
            left = edges[0, :, pl.ds(pl.multiple_of(q * 128, 128), 128)]
            total = dot(jnp.transpose(left.astype(F32)).astype(BF16), edges[1])
            for half in range(2):
                for a in range(OWN):
                    for k2 in range(2):
                        for b in range(4):
                            at = (k2 * CHIPS + (2 * q + half) * 8) * 16 + a * 4 + b
                            row = half * 64 + a * 16 + k2 * 8
                            wide[pl.ds(at, 8, stride=16), :] = total[
                                row : row + 8, b * 128 : (b + 1) * 128
                            ]

        send_b[t] = wide[0:2048, :].reshape(128, 16, 128).astype(BF16)
        send_far(send_b.at[t], recv_b.at[t], k + 1, (0, 1))
        send_near(send_b.at[t], recv_b.at[t], k + 1)

    def gates(t):
        for a in range(OWN):
            gate_cm[a] = jax.nn.sigmoid(dot(wt_in[t, 4 * C : 5 * C, :], norm8[a]))

    def finish(t, k, then):
        arrived(recv_b.at[t], k)
        wide[0:2048, :] = recv_b[t].astype(F32).reshape(2048, 128)

        @pl.loop(0, OWN)
        def _(a):
            total = jnp.concatenate(
                [wide[pl.ds(a * 4 + b, 128, stride=16), :] for b in range(4)], axis=1
            )
            normed = norm_cm(total, jnp.tile(gain_b[2 * t + 1], (1, 4))).astype(BF16)
            update = gate_cm[a] * dot(wt_out[t], normed)
            new = (pair_cm[a] + update).astype(BF16).astype(F32)
            pair_cm[a] = new
            then(a, norm_cm(new, jnp.tile(gain_b[2 * t + 2], (1, 4))).astype(BF16))

    triangle(0, 1)

    arrived(rows_in, 0)

    @pl.loop(0, OWN)
    def _(a):
        x = jnp.transpose(rows_in[a].astype(F32))
        pair_cm[a] = x
        norm8[a] = norm_cm(x, jnp.tile(gain_b[0], (1, 4))).astype(BF16)

    gates(0)

    def keep_norm(a, normed):
        norm8[a] = normed

    finish(0, 2, keep_norm)

    for half in range(2):

        @pl.loop(2 * half, 2 * half + 2)
        def _(step):
            make_edges(1, pl.multiple_of(step * 32, 32), norm8, keep8)

        send_far(send_a.at[1], recv_a.at[1], 3, (half,))
    send_near(send_a.at[1], recv_a.at[1], 3)
    gates(1)
    triangle(1, 3)

    sibling = (r, duo * 2 + other)
    own_half = pl.multiple_of(core * HALF, HALF)

    def bias_part(a, normed):
        norm8[a] = normed
        bias = dot(w_bias[...], normed)
        for h in range(H):
            for kb in range(4):
                wide[pl.ds(2048 + h * 16 + kb * 4 + a, 1), :] = bias[
                    h : h + 1, kb * 128 : (kb + 1) * 128
                ]
        half_send[a] = pair_cm[a, :, pl.ds(pl.multiple_of(other * HALF, HALF), HALF)].astype(BF16)
        resid8[a] = pair_cm[a, :, pl.ds(own_half, HALF)].astype(BF16)

    finish(1, 4, bias_part)
    bias_send[...] = wide[2048 : 2048 + 64, :].reshape(H, 16, 128).astype(BF16)

    asks = lax.div(r, 4)
    slot = cy * 16 + place
    for h in range(H):

        def visit(r2, duo2):
            pltpu.make_async_remote_copy(
                bias_send.at[h],
                bias_recv.at[h, slot],
                sem_send.at[5],
                sem_recv.at[5 + h],
                device_id=(r2, duo2 * 2 + asks),
                device_id_type=MESH,
            ).start()

        far_chips(visit)

        @pl.when(asks == core)
        def _():
            pltpu.make_async_copy(
                bias_send.at[h], bias_recv.at[h, slot], sem_recv.at[5 + h]
            ).start()

        @pl.when(asks != core)
        def _():
            pltpu.make_async_remote_copy(
                bias_send.at[h],
                bias_recv.at[h, slot],
                sem_send.at[5],
                sem_recv.at[5 + h],
                device_id=sibling,
                device_id_type=MESH,
            ).start()

        if h == 0:
            pltpu.make_async_remote_copy(
                norm8.at[pl.ds(0, OWN)],
                norm8.at[pl.ds(OWN, OWN)],
                sem_send.at[6],
                sem_recv.at[9],
                device_id=sibling,
                device_id_type=MESH,
            ).start()
            pltpu.make_async_remote_copy(
                half_send,
                resid8.at[pl.ds(OWN, OWN)],
                sem_send.at[7],
                sem_recv.at[10],
                device_id=sibling,
                device_id_type=MESH,
            ).start()

    lane_q = lax.broadcasted_iota(jnp.int32, (HALF, C), 1)
    lane_v = lax.broadcasted_iota(jnp.int32, (N, C), 1)
    first_lane = jnp.where(lane_q == 0, 1.0, 0.0).astype(BF16)
    first_row = lax.broadcasted_iota(jnp.int32, (C, N), 0) == 0

    def prepare(i):
        k_ext[i, 0:C, :] = dot(wt_k[...], norm8[i]).astype(BF16)
        penalty = jnp.where(keep8[pl.ds(i, 1), :] > 0.5, 0.0, -1e9)
        k_ext[i, C:, :] = jnp.where(first_row, penalty, 0.0).astype(BF16)
        rows_in[0] = jnp.transpose(norm8[i].astype(F32)).astype(BF16)
        values = dot(rows_in[0], w_attn[:, 2 * C : 3 * C])
        asked = rows_in[0, pl.ds(own_half, HALF), :]
        queries = dot(asked, w_attn[:, 0:C]) * (32**-0.5 * LOG2E)
        gate8[i] = jax.nn.sigmoid(dot(asked, w_attn[:, 3 * C :]))
        for h in range(H):
            here_q = jnp.logical_and(lane_q >= 32 * h, lane_q < 32 * (h + 1))
            here_v = jnp.logical_and(lane_v >= 32 * h, lane_v < 32 * (h + 1))
            q_ext[i, h, :, 0:C] = jnp.where(here_q, queries, 0.0).astype(BF16)
            q_ext[i, h, :, C:] = first_lane
            v_ext[i, h, :, 0:C] = jnp.where(here_v, values, 0.0).astype(BF16)
            v_ext[i, h, :, C:] = jnp.ones((N, C), BF16)

    pl.loop(0, OWN)(prepare)
    arrived(norm8.at[pl.ds(OWN, OWN)], 9)
    pl.loop(OWN, 2 * OWN)(prepare)
    arrived(resid8.at[pl.ds(OWN, OWN)], 10)

    for h in range(H):
        arrived(bias_recv.at[h], 5 + h)
        wide[0:1024, :] = bias_recv[h].astype(F32).reshape(1024, 128) * LOG2E
        for y in range(4):
            for a in range(OWN):
                for kb in range(4):
                    bias_nat[
                        y * 64 + a * 16 : y * 64 + a * 16 + 16, kb * 128 : (kb + 1) * 128
                    ] = wide[pl.ds(y * 256 + kb * 4 + a, 16, stride=16), :]

        @pl.loop(0, 2 * OWN)
        def _(i):
            scores = dot(q_ext[i, h], k_ext[i]) + bias_nat[...]
            mixed = dot(jnp.exp2(scores).astype(BF16), v_ext[i, h])
            part = mixed[:, 0:C] / mixed[:, C:]
            if h == 0:
                total8[i] = part
            elif h < H - 1:
                total8[i] += part
            else:
                gated = (gate8[i] * (total8[i] + part)).astype(BF16)
                update = dot(gated, w_final[...])
                rows_out[i] = (jnp.transpose(resid8[i].astype(F32)) + update).astype(BF16)
                a = lax.rem(i, OWN)
                owner = lax.rem(core + lax.div(i, OWN), 2) * 8 + duo

                @pl.loop(0, 8)
                def _(u):
                    source = rows_out.at[i, pl.ds(u * 32, 32)]
                    target = out.at[a, owner]

                    @pl.when(core * 8 + u == c)
                    def _():
                        pltpu.make_async_copy(source, target, sem_recv.at[11]).start()

                    @pl.when(core * 8 + u != c)
                    def _():
                        pltpu.make_async_remote_copy(
                            source,
                            target,
                            sem_send.at[8],
                            sem_recv.at[11],
                            device_id=(r, core * 8 + u),
                            device_id_type=MESH,
                        ).start()

    arrived(out, 11)

    sent(out.at[:, pl.ds(0, COLS - 1)], 0)
    for t in range(2):
        sent(recv_a.at[t, pl.ds(0, DEV - 1)], 2 * t + 1)
        sent(recv_b.at[t, pl.ds(0, DEV - 1)], 2 * t + 2)
    sent(norm8.at[pl.ds(0, OWN)], 6)
    sent(half_send, 7)

    @pl.when(asks == core)
    def _():
        sent(bias_recv.at[:, pl.ds(0, CHIPS - 1)], 5)

    @pl.when(asks != core)
    def _():
        sent(bias_recv, 5)

    @pl.when(lax.div(c, 8) == core)
    def _():
        sent(out.at[:, pl.ds(0, COLS - 2)], 8)

    @pl.when(lax.div(c, 8) != core)
    def _():
        sent(out, 8)


def per_device(
    pair, chain_id, block_mask, norm_gains, w_in, w_out, w_attn, w_bias, w_final
):
    vmem = pl.BlockSpec(memory_space=pltpu.VMEM)
    smem = pl.BlockSpec(memory_space=pltpu.SMEM)
    result = pl.pallas_call(
        kernel,
        out_shape=jax.ShapeDtypeStruct((OWN, COLS, 32, C), BF16),
        in_specs=[vmem, smem, vmem, smem] + [vmem] * 6,
        out_specs=vmem,
        scratch_shapes=[
            pltpu.VMEM((OWN, N, C), BF16),
            pltpu.VMEM((OWN, C, N), F32),
            pltpu.VMEM((OWN, C, N), F32),
            pltpu.VMEM((2 * OWN, C, N), BF16),
            pltpu.VMEM((OWN, C, N), BF16),
            pltpu.VMEM((2 * OWN, N), F32),
            pltpu.VMEM((8, N), F32),
            pltpu.VMEM((5, C, C), F32),
            pltpu.VMEM((2, 5 * C, C), BF16),
            pltpu.VMEM((2, C, C), BF16),
            pltpu.VMEM((C, C), BF16),
            pltpu.VMEM((4096, C), F32),
            pltpu.VMEM((2, N, N), BF16),
            pltpu.VMEM((2, DEV, 32, C), BF16),
            pltpu.VMEM((2, DEV, 32, C), BF16),
            pltpu.VMEM((2, DEV, 16, C), BF16),
            pltpu.VMEM((2, DEV, 16, C), BF16),
            pltpu.VMEM((H, 16, C), BF16),
            pltpu.VMEM((H, CHIPS, 16, C), BF16),
            pltpu.VMEM((HALF, N), F32),
            pltpu.VMEM((OWN, C, HALF), BF16),
            pltpu.VMEM((2 * OWN, C, HALF), BF16),
            pltpu.VMEM((2 * OWN, H, HALF, 2 * C), BF16),
            pltpu.VMEM((2 * OWN, 2 * C, N), BF16),
            pltpu.VMEM((2 * OWN, H, N, 2 * C), BF16),
            pltpu.VMEM((2 * OWN, HALF, C), F32),
            pltpu.VMEM((2 * OWN, HALF, C), F32),
            pltpu.VMEM((2 * OWN, HALF, C), BF16),
            pltpu.SemaphoreType.DMA((9,)),
            pltpu.SemaphoreType.DMA((12,)),
        ],
        name="triangle_block",
        compiler_params=pltpu.CompilerParams(
            collective_id=0, has_side_effects=True, vmem_limit_bytes=60 << 20
        ),
        cost_estimate=pl.CostEstimate(
            flops=3 * 10**9, bytes_accessed=2 * 10**6, transcendentals=5 * 10**6
        ),
    )(
        pair.reshape(OWN, COLS, 32, C),
        chain_id,
        chain_id.reshape(1, N),
        block_mask,
        norm_gains,
        w_in,
        w_out,
        w_attn,
        w_bias.T,
        w_final,
    )
    return result.reshape(64, 32, C)


def solution(mesh):
    placed = (P("row", "col", None), P(), P(), P(), P(), P(), P(), P(), P())
    return jax.shard_map(
        per_device, mesh=mesh, in_specs=placed, out_specs=P("row", "col", None), check_vma=False
    )
```

time: 145 us -> 108 us (0.74)
  Pallas kernels: 141 us -> 106 us
    pallas_call x1, Pallas kernels: 141 us -> 106 us  [per_device(): pl.pallas_call(kernel, out_shape=jax.ShapeDtypeStruct((OWN, COLS, 32, C),...]
where the time goes in v2:
time: 108 us
  Pallas kernels  106 us (98%)
  local copies, waits for them, and re-layouts  1.87 us (2%)
    pallas_call x1, Pallas kernels, per_device(): pl.pallas_call(kernel, out_shape=jax.ShapeDtypeStruct((OWN, COLS, 32, C),...  106 us

profile of v2, /device:TPU:1, one launch (start us, length us, event | category | flops | bytes accessed | tf_op | source)
XLA Modules:
  0.0 107.8 jit_solution(14815505388028798140)
XLA Ops:
  0.0 105.9 %triangle_block.1 = bf16[4,16,32,128]{3,2,1,0:T(8,128)(2,1)} custom-call(bf16[4,16,32,128]{3,2,1,0:T(8,128)(2,1)} %bitcast.5, s32[512]{0:T(512)} %chain_s.1, s32[1,512]{1,0:T(1,128)} %bitcast.6, s32[8,8]{1,0:T(8,128)} %block_s.1, f32[5,128]{1,0:T(8,128)} %gains.1, bf16[2,128,640]{2,1,0:T(8,128)(2,1)} %w_in.1, bf16[2,128,128]{2,1,0:T(8,128)(2,1)} %w_out.1, ...), custom_call_target="tpu_custom_call" | custom-call | flops 3000000000 | bytes 2000000 | tf_op jit(solution)/shard_map/triangle_block/pallas_call | solution.py:511
  105.9 1.9 %copy.11 = bf16[64,32,128]{2,1,0:T(8,128)(2,1)} copy(bf16[64,32,128]{2,1,0:T(8,128)(2,1)} %bitcast.4) | data formatting | bytes 1048576

commit v3 on v2

--- a/solution.py
+++ b/solution.py
@@ -38,6 +38,11 @@
 
 def dot(a, b):
     return jnp.dot(a, b, preferred_element_type=F32)
+
+
+def inverse(x):
+    guess = pltpu.reciprocal(x, approx=True)
+    return guess * (2.0 - x * guess)
 
 
 def norm_cm(x, gain):
@@ -163,27 +168,19 @@
                     wide[pl.ds(base * 32 + side * 16 + a * 4 + b, 32, stride=32), :] = e[
                         :, b * 128 : (b + 1) * 128
                     ]
-        part = wide[pl.ds(pl.multiple_of(base * 32, 1024), 1024), :]
-        send_a[t, pl.ds(base, 32)] = part.reshape(32, 32, 128).astype(BF16)
-
-    for n in range(5):
-        gain_b[n] = jnp.transpose(jnp.broadcast_to(gains[n : n + 1, :], (C, C)))
-    for t in range(2):
+        part = wide[base * 32 : base * 32 + 1024, :]
+        send_a[t, base : base + 32] = part.reshape(32, 32, 128).astype(BF16)
+
+    def set_in(t):
         for g in range(5):
             part = w_in[t, :, g * C : (g + 1) * C].astype(F32)
             wt_in[t, g * C : (g + 1) * C, :] = jnp.transpose(part).astype(BF16)
-        wt_out[t] = jnp.transpose(w_out[t].astype(F32)).astype(BF16)
-    wt_k[...] = jnp.transpose(w_attn[:, C : 2 * C].astype(F32)).astype(BF16)
-
-    block_of = lax.broadcasted_iota(jnp.int32, (1, N), 1) // 64
-    linked = jnp.zeros((1, N), jnp.int32)
-    for nb in range(8):
-        linked = jnp.where(block_of == nb, block_s[r, nb], linked)
-    for i in range(2 * OWN):
-        at = place if i < OWN else other * 8 + duo
-        own_chain = chain_s[r * 64 + (i % OWN) * 16 + at]
-        allowed = jnp.logical_or(chain_v[...] == own_chain, linked == 1)
-        keep8[i : i + 1, :] = jnp.where(allowed, 1.0, 0.0).astype(F32)
+
+    def set_gain(n):
+        gain_b[n] = jnp.transpose(jnp.broadcast_to(gains[n : n + 1, :], (C, C)))
+
+    set_in(0)
+    set_gain(0)
 
     lane = lax.broadcasted_iota(jnp.int32, (1, C), 1)
     row_of = lax.rem(lane, 64)
@@ -202,8 +199,7 @@
 
     wide[0:2048, :] = pair[...].astype(F32).reshape(2048, C)
 
-    @pl.loop(0, 4)
-    def _(a):
+    for a in range(4):
         for b in range(4):
             s = a * 4 + b
             x = jnp.concatenate(
@@ -213,13 +209,12 @@
                 BF16
             )
 
-    @pl.loop(0, 4)
-    def _(step):
-        make_edges(0, pl.multiple_of(step * 32, 32), norm_0, keep_0)
-
-    pl.semaphore_wait(barrier, DEV - 1)
-
-    send_far(send_a.at[0], recv_a.at[0], 1, (0, 1))
+    for half in range(2):
+        for step in (2 * half, 2 * half + 1):
+            make_edges(0, step * 32, norm_0, keep_0)
+        if half == 0:
+            pl.semaphore_wait(barrier, DEV - 1)
+        send_far(send_a.at[0], recv_a.at[0], 1, (half,))
     send_near(send_a.at[0], recv_a.at[0], 1)
 
     pltpu.make_async_copy(
@@ -238,21 +233,36 @@
             device_id_type=MESH,
         ).start()
 
+    for n in range(1, 5):
+        set_gain(n)
+    set_in(1)
+    for t in range(2):
+        wt_out[t] = jnp.transpose(w_out[t].astype(F32)).astype(BF16)
+    wt_k[...] = jnp.transpose(w_attn[:, C : 2 * C].astype(F32)).astype(BF16)
+
+    block_of = lax.broadcasted_iota(jnp.int32, (1, N), 1) // 64
+    linked = jnp.zeros((1, N), jnp.int32)
+    for nb in range(8):
+        linked = jnp.where(block_of == nb, block_s[r, nb], linked)
+    for i in range(2 * OWN):
+        at = place if i < OWN else other * 8 + duo
+        own_chain = chain_s[r * 64 + (i % OWN) * 16 + at]
+        allowed = jnp.logical_or(chain_v[...] == own_chain, linked == 1)
+        keep8[i : i + 1, :] = jnp.where(allowed, 1.0, 0.0).astype(F32)
+
     def triangle(t, k):
         arrived(recv_a.at[t], k)
         if t == 0:
             low = lax.broadcasted_iota(jnp.int32, (C, C), 1) < 64
             for side in range(2):
                 for q in range(4):
-
-                    @pl.loop(0, 2)
-                    def _(k2):
+                    for k2 in range(2):
                         first = k2 * CHIPS + 2 * q * 8
                         here = recv_a[t, pl.ds(first, 8), side * 16 : side * 16 + 16]
                         there = recv_a[t, pl.ds(first + 8, 8), side * 16 : side * 16 + 16]
                         here = here.astype(F32).reshape(C, C)
                         there = there.astype(F32).reshape(C, C)
-                        at = pl.multiple_of(k2 * 128, 128)
+                        at = k2 * 128
                         edges[side, pl.ds(at, 128), q * 128 : (q + 1) * 128] = jnp.where(
                             low, here, pltpu.roll(there, 64, 1)
                         ).astype(BF16)
@@ -263,17 +273,14 @@
             wide[...] = recv_a[t].astype(F32).reshape(4096, 128)
             for side in range(2):
                 for b in range(4):
-
-                    @pl.loop(0, OWN)
-                    def _(a):
+                    for a in range(OWN):
                         block = wide[pl.ds(side * 16 + a * 4 + b, 128, stride=32), :]
                         edges[
-                            side, pl.ds(pl.multiple_of(a * 128, 128), 128), b * 128 : (b + 1) * 128
+                            side, a * 128 : (a + 1) * 128, b * 128 : (b + 1) * 128
                         ] = block.astype(BF16)
 
-        @pl.loop(0, 4)
-        def _(q):
-            left = edges[0, :, pl.ds(pl.multiple_of(q * 128, 128), 128)]
+        for q in range(4):
+            left = edges[0, :, q * 128 : (q + 1) * 128]
             total = dot(jnp.transpose(left.astype(F32)).astype(BF16), edges[1])
             for half in range(2):
                 for a in range(OWN):
@@ -297,8 +304,7 @@
         arrived(recv_b.at[t], k)
         wide[0:2048, :] = recv_b[t].astype(F32).reshape(2048, 128)
 
-        @pl.loop(0, OWN)
-        def _(a):
+        for a in range(OWN):
             total = jnp.concatenate(
                 [wide[pl.ds(a * 4 + b, 128, stride=16), :] for b in range(4)], axis=1
             )
@@ -311,9 +317,7 @@
     triangle(0, 1)
 
     arrived(rows_in, 0)
-
-    @pl.loop(0, OWN)
-    def _(a):
+    for a in range(OWN):
         x = jnp.transpose(rows_in[a].astype(F32))
         pair_cm[a] = x
         norm8[a] = norm_cm(x, jnp.tile(gain_b[0], (1, 4))).astype(BF16)
@@ -326,10 +330,8 @@
     finish(0, 2, keep_norm)
 
     for half in range(2):
-
-        @pl.loop(2 * half, 2 * half + 2)
-        def _(step):
-            make_edges(1, pl.multiple_of(step * 32, 32), norm8, keep8)
+        for step in (2 * half, 2 * half + 1):
+            make_edges(1, step * 32, norm8, keep8)
 
         send_far(send_a.at[1], recv_a.at[1], 3, (half,))
     send_near(send_a.at[1], recv_a.at[1], 3)
@@ -431,6 +433,21 @@
     pl.loop(OWN, 2 * OWN)(prepare)
     arrived(resid8.at[pl.ds(OWN, OWN)], 10)
 
+    def out_part(i, u):
+        owner = (core if i < OWN else other) * 8 + duo
+        return rows_out.at[i, pl.ds(pl.multiple_of(u * 32, 32), 32)], out.at[i % OWN, owner]
+
+    def send_out(i, u):
+        source, target = out_part(i, u)
+        pltpu.make_async_remote_copy(
+            source,
+            target,
+            sem_send.at[8],
+            sem_recv.at[11],
+            device_id=(r, core * 8 + u),
+            device_id_type=MESH,
+        ).start()
+
     for h in range(H):
         arrived(bias_recv.at[h], 5 + h)
         wide[0:1024, :] = bias_recv[h].astype(F32).reshape(1024, 128) * LOG2E
@@ -441,11 +458,10 @@
                         y * 64 + a * 16 : y * 64 + a * 16 + 16, kb * 128 : (kb + 1) * 128
                     ] = wide[pl.ds(y * 256 + kb * 4 + a, 16, stride=16), :]
 
-        @pl.loop(0, 2 * OWN)
-        def _(i):
+        for i in range(2 * OWN):
             scores = dot(q_ext[i, h], k_ext[i]) + bias_nat[...]
             mixed = dot(jnp.exp2(scores).astype(BF16), v_ext[i, h])
-            part = mixed[:, 0:C] / mixed[:, C:]
+            part = mixed[:, 0:C] * inverse(mixed[:, C:])
             if h == 0:
                 total8[i] = part
             elif h < H - 1:
@@ -454,28 +470,19 @@
                 gated = (gate8[i] * (total8[i] + part)).astype(BF16)
                 update = dot(gated, w_final[...])
                 rows_out[i] = (jnp.transpose(resid8[i].astype(F32)) + update).astype(BF16)
-                a = lax.rem(i, OWN)
-                owner = lax.rem(core + lax.div(i, OWN), 2) * 8 + duo
-
-                @pl.loop(0, 8)
-                def _(u):
-                    source = rows_out.at[i, pl.ds(u * 32, 32)]
-                    target = out.at[a, owner]
-
-                    @pl.when(core * 8 + u == c)
-                    def _():
-                        pltpu.make_async_copy(source, target, sem_recv.at[11]).start()
-
-                    @pl.when(core * 8 + u != c)
-                    def _():
-                        pltpu.make_async_remote_copy(
-                            source,
-                            target,
-                            sem_send.at[8],
-                            sem_recv.at[11],
-                            device_id=(r, core * 8 + u),
-                            device_id_type=MESH,
-                        ).start()
+                for u in range(1, 8):
+                    send_out(i, lax.rem(c + u, 8))
+
+    @pl.when(lax.div(c, 8) == core)
+    def _():
+        for i in range(2 * OWN):
+            source, target = out_part(i, lax.rem(c, 8))
+            pltpu.make_async_copy(source, target, sem_recv.at[11]).start()
+
+    @pl.when(lax.div(c, 8) != core)
+    def _():
+        for i in range(2 * OWN):
+            send_out(i, lax.rem(c, 8))
 
     arrived(out, 11)
 

time: 108 us -> 97.3 us (0.901)
  Pallas kernels: 106 us -> 95.3 us
    pallas_call x1, Pallas kernels: 106 us -> 95.3 us  [per_device(): pl.pallas_call(kernel, out_shape=jax.ShapeDtypeStruct((OWN, COLS, 32, C),...]
where the time goes in v3:
time: 97.3 us; the launch traced here: 97.2 us
  Pallas kernels  95.3 us (98%)
  local copies, waits for them, and re-layouts  1.87 us (2%)
    pallas_call x1, Pallas kernels, per_device(): pl.pallas_call(kernel, out_shape=jax.ShapeDtypeStruct((OWN, COLS, 32, C),...  95.3 us

profile of v3, /device:TPU:1, one launch (start us, length us, event | category | flops | bytes accessed | tf_op | source)
XLA Modules:
  0.0 97.2 jit_solution(6673538401663447417)
XLA Ops:
  0.0 95.3 %triangle_block.1 = bf16[4,16,32,128]{3,2,1,0:T(8,128)(2,1)} custom-call(bf16[4,16,32,128]{3,2,1,0:T(8,128)(2,1)} %bitcast.5, s32[512]{0:T(512)} %chain_s.1, s32[1,512]{1,0:T(1,128)} %bitcast.6, s32[8,8]{1,0:T(8,128)} %block_s.1, f32[5,128]{1,0:T(8,128)} %gains.1, bf16[2,128,640]{2,1,0:T(8,128)(2,1)} %w_in.1, bf16[2,128,128]{2,1,0:T(8,128)(2,1)} %w_out.1, ...), custom_call_target="tpu_custom_call" | custom-call | flops 3000000000 | bytes 2000000 | tf_op jit(solution)/shard_map/triangle_block/pallas_call | solution.py:518
  95.3 1.9 %copy.11 = bf16[64,32,128]{2,1,0:T(8,128)(2,1)} copy(bf16[64,32,128]{2,1,0:T(8,128)(2,1)} %bitcast.4) | data formatting | bytes 1048576

commit v4 on v3

--- a/solution.py
+++ b/solution.py
@@ -108,12 +108,21 @@
 
     barrier = pltpu.get_barrier_semaphore()
 
-    @pl.loop(1, DEV)
-    def _(step):
-        t = lax.rem(r * COLS + c + step, DEV)
+    def greet(i, j):
         pl.semaphore_signal(
-            barrier, inc=1, device_id=(lax.div(t, COLS), lax.rem(t, COLS)), device_id_type=MESH
+            barrier,
+            inc=1,
+            device_id=(lax.rem(r + i, ROWS), lax.rem(c + j, COLS)),
+            device_id_type=MESH,
         )
+
+    for j in range(1, COLS):
+        greet(0, j)
+
+    @pl.loop(1, ROWS)
+    def _(i):
+        for j in range(COLS):
+            greet(i, j)
 
     def far_chips(visit):
         for packed, count in FAR:
@@ -292,8 +301,10 @@
                                 row : row + 8, b * 128 : (b + 1) * 128
                             ]
 
-        send_b[t] = wide[0:2048, :].reshape(128, 16, 128).astype(BF16)
-        send_far(send_b.at[t], recv_b.at[t], k + 1, (0, 1))
+        for k2 in range(2):
+            part = wide[k2 * 1024 : (k2 + 1) * 1024, :].reshape(CHIPS, 16, 128)
+            send_b[t, k2 * CHIPS : (k2 + 1) * CHIPS] = part.astype(BF16)
+            send_far(send_b.at[t], recv_b.at[t], k + 1, (k2,))
         send_near(send_b.at[t], recv_b.at[t], k + 1)
 
     def gates(t):
@@ -351,14 +362,26 @@
                 ]
         half_send[a] = pair_cm[a, :, pl.ds(pl.multiple_of(other * HALF, HALF), HALF)].astype(BF16)
         resid8[a] = pair_cm[a, :, pl.ds(own_half, HALF)].astype(BF16)
+        for source, target, k in (
+            (norm8.at[a], norm8.at[OWN + a], 6),
+            (half_send.at[a], resid8.at[OWN + a], 7),
+        ):
+            pltpu.make_async_remote_copy(
+                source,
+                target,
+                sem_send.at[k],
+                sem_recv.at[k + 3],
+                device_id=sibling,
+                device_id_type=MESH,
+            ).start()
 
     finish(1, 4, bias_part)
     bias_send[...] = wide[2048 : 2048 + 64, :].reshape(H, 16, 128).astype(BF16)
 
     asks = lax.div(r, 4)
     slot = cy * 16 + place
-    for h in range(H):
-
+
+    def send_bias(h):
         def visit(r2, duo2):
             pltpu.make_async_remote_copy(
                 bias_send.at[h],
@@ -379,32 +402,7 @@
 
         @pl.when(asks != core)
         def _():
-            pltpu.make_async_remote_copy(
-                bias_send.at[h],
-                bias_recv.at[h, slot],
-                sem_send.at[5],
-                sem_recv.at[5 + h],
-                device_id=sibling,
-                device_id_type=MESH,
-            ).start()
-
-        if h == 0:
-            pltpu.make_async_remote_copy(
-                norm8.at[pl.ds(0, OWN)],
-                norm8.at[pl.ds(OWN, OWN)],
-                sem_send.at[6],
-                sem_recv.at[9],
-                device_id=sibling,
-                device_id_type=MESH,
-            ).start()
-            pltpu.make_async_remote_copy(
-                half_send,
-                resid8.at[pl.ds(OWN, OWN)],
-                sem_send.at[7],
-                sem_recv.at[10],
-                device_id=sibling,
-                device_id_type=MESH,
-            ).start()
+            visit(r, duo)
 
     lane_q = lax.broadcasted_iota(jnp.int32, (HALF, C), 1)
     lane_v = lax.broadcasted_iota(jnp.int32, (N, C), 1)
@@ -413,7 +411,7 @@
 
     def prepare(i):
         k_ext[i, 0:C, :] = dot(wt_k[...], norm8[i]).astype(BF16)
-        penalty = jnp.where(keep8[pl.ds(i, 1), :] > 0.5, 0.0, -1e9)
+        penalty = jnp.where(keep8[i : i + 1, :] > 0.5, 0.0, -1e9)
         k_ext[i, C:, :] = jnp.where(first_row, penalty, 0.0).astype(BF16)
         rows_in[0] = jnp.transpose(norm8[i].astype(F32)).astype(BF16)
         values = dot(rows_in[0], w_attn[:, 2 * C : 3 * C])
@@ -428,9 +426,12 @@
             v_ext[i, h, :, 0:C] = jnp.where(here_v, values, 0.0).astype(BF16)
             v_ext[i, h, :, C:] = jnp.ones((N, C), BF16)
 
-    pl.loop(0, OWN)(prepare)
-    arrived(norm8.at[pl.ds(OWN, OWN)], 9)
-    pl.loop(OWN, 2 * OWN)(prepare)
+    for h in range(H):
+        send_bias(h)
+        if h == 2:
+            arrived(norm8.at[pl.ds(OWN, OWN)], 9)
+        prepare(2 * h)
+        prepare(2 * h + 1)
     arrived(resid8.at[pl.ds(OWN, OWN)], 10)
 
     def out_part(i, u):
@@ -517,7 +518,7 @@
     smem = pl.BlockSpec(memory_space=pltpu.SMEM)
     result = pl.pallas_call(
         kernel,
-        out_shape=jax.ShapeDtypeStruct((OWN, COLS, 32, C), BF16),
+        out_shape=pltpu.VMEM((OWN, COLS, 32, C), BF16),
         in_specs=[vmem, smem, vmem, smem] + [vmem] * 6,
         out_specs=vmem,
         scratch_shapes=[

time: 97.3 us -> 94.6 us (0.972)
  Pallas kernels: 95.3 us -> 93.7 us
  local copies, waits for them, and re-layouts: 1.87 us -> 0.8 us
    pallas_call x1, Pallas kernels: 95.3 us -> 93.7 us  [per_device(): pl.pallas_call(kernel, out_shape=pltpu.VMEM((OWN, COLS, 32, C), BF16), in...]
    unnamed x1, local copies, waits for them, and re-layouts: 1.87 us -> 0.8 us
where the time goes in v4:
time: 94.6 us; the launch traced here: 94.5 us
  Pallas kernels  93.7 us (99%)
    pallas_call x1, Pallas kernels, per_device(): pl.pallas_call(kernel, out_shape=pltpu.VMEM((OWN, COLS, 32, C), BF16), in...  93.7 us

profile of v4, /device:TPU:1, one launch (start us, length us, event | category | flops | bytes accessed | tf_op | source)
XLA Modules:
  0.0 94.5 jit_solution(12079037715519543032)
XLA Ops:
  0.0 93.7 %triangle_block.1 = bf16[4,16,32,128]{3,2,1,0:T(8,128)(2,1)S(1)} custom-call(bf16[4,16,32,128]{3,2,1,0:T(8,128)(2,1)} %bitcast.5, s32[512]{0:T(512)} %chain_s.1, s32[1,512]{1,0:T(1,128)} %bitcast.6, s32[8,8]{1,0:T(8,128)} %block_s.1, f32[5,128]{1,0:T(8,128)} %gains.1, bf16[2,128,640]{2,1,0:T(8,128)(2,1)} %w_in.1, bf16[2,128,128]{2,1,0:T(8,128)(2,1)} %w_out.1, ...), custom_call_target="tpu_custom_call" | custom-call | flops 3000000000 | bytes 2000000 | tf_op jit(solution)/shard_map/triangle_block/pallas_call | solution.py:519
  93.7 0.8 copy.11

commit v5 on v4

--- a/solution.py
+++ b/solution.py
@@ -43,6 +43,10 @@
 def inverse(x):
     guess = pltpu.reciprocal(x, approx=True)
     return guess * (2.0 - x * guess)
+
+
+def sigmoid(x):
+    return 0.5 * jnp.tanh(0.5 * x) + 0.5
 
 
 def norm_cm(x, gain):
@@ -119,8 +123,7 @@
     for j in range(1, COLS):
         greet(0, j)
 
-    @pl.loop(1, ROWS)
-    def _(i):
+    for i in range(1, ROWS):
         for j in range(COLS):
             greet(i, j)
 
@@ -172,7 +175,7 @@
             for side in range(2):
                 g = dot(wt_in[t, pl.ds(2 * side * C + base, 32), :], x)
                 v = dot(wt_in[t, pl.ds((2 * side + 1) * C + base, 32), :], x)
-                e = jax.nn.sigmoid(g) * v * m
+                e = sigmoid(g) * v * m
                 for b in range(4):
                     wide[pl.ds(base * 32 + side * 16 + a * 4 + b, 32, stride=32), :] = e[
                         :, b * 128 : (b + 1) * 128
@@ -309,7 +312,7 @@
 
     def gates(t):
         for a in range(OWN):
-            gate_cm[a] = jax.nn.sigmoid(dot(wt_in[t, 4 * C : 5 * C, :], norm8[a]))
+            gate_cm[a] = sigmoid(dot(wt_in[t, 4 * C : 5 * C, :], norm8[a]))
 
     def finish(t, k, then):
         arrived(recv_b.at[t], k)
@@ -362,20 +365,20 @@
                 ]
         half_send[a] = pair_cm[a, :, pl.ds(pl.multiple_of(other * HALF, HALF), HALF)].astype(BF16)
         resid8[a] = pair_cm[a, :, pl.ds(own_half, HALF)].astype(BF16)
-        for source, target, k in (
-            (norm8.at[a], norm8.at[OWN + a], 6),
-            (half_send.at[a], resid8.at[OWN + a], 7),
-        ):
-            pltpu.make_async_remote_copy(
-                source,
-                target,
-                sem_send.at[k],
-                sem_recv.at[k + 3],
-                device_id=sibling,
-                device_id_type=MESH,
-            ).start()
 
     finish(1, 4, bias_part)
+    for source, target, k in (
+        (norm8.at[pl.ds(0, OWN)], norm8.at[pl.ds(OWN, OWN)], 6),
+        (half_send, resid8.at[pl.ds(OWN, OWN)], 7),
+    ):
+        pltpu.make_async_remote_copy(
+            source,
+            target,
+            sem_send.at[k],
+            sem_recv.at[k + 3],
+            device_id=sibling,
+            device_id_type=MESH,
+        ).start()
     bias_send[...] = wide[2048 : 2048 + 64, :].reshape(H, 16, 128).astype(BF16)
 
     asks = lax.div(r, 4)
@@ -417,7 +420,7 @@
         values = dot(rows_in[0], w_attn[:, 2 * C : 3 * C])
         asked = rows_in[0, pl.ds(own_half, HALF), :]
         queries = dot(asked, w_attn[:, 0:C]) * (32**-0.5 * LOG2E)
-        gate8[i] = jax.nn.sigmoid(dot(asked, w_attn[:, 3 * C :]))
+        gate8[i] = sigmoid(dot(asked, w_attn[:, 3 * C :]))
         for h in range(H):
             here_q = jnp.logical_and(lane_q >= 32 * h, lane_q < 32 * (h + 1))
             here_v = jnp.logical_and(lane_v >= 32 * h, lane_v < 32 * (h + 1))
@@ -471,8 +474,10 @@
                 gated = (gate8[i] * (total8[i] + part)).astype(BF16)
                 update = dot(gated, w_final[...])
                 rows_out[i] = (jnp.transpose(resid8[i].astype(F32)) + update).astype(BF16)
-                for u in range(1, 8):
-                    send_out(i, lax.rem(c + u, 8))
+                if i % 2 == 1:
+                    for row in range(i - 1, i + 1):
+                        for u in range(1, 8):
+                            send_out(row, lax.rem(c + u, 8))
 
     @pl.when(lax.div(c, 8) == core)
     def _():

time: 94.6 us -> 94.3 us (level)
  no operation moved by 1% of the time
where the time goes in v5:
time: 94.3 us; the launch traced here: 94.2 us
  Pallas kernels  93.4 us (99%)
    pallas_call x1, Pallas kernels, per_device(): pl.pallas_call(kernel, out_shape=pltpu.VMEM((OWN, COLS, 32, C), BF16), in...  93.4 us

profile of v5, /device:TPU:1, one launch (start us, length us, event | category | flops | bytes accessed | tf_op | source)
XLA Modules:
  0.0 94.2 jit_solution(15911768481469096016)
XLA Ops:
  0.0 93.4 %triangle_block.1 = bf16[4,16,32,128]{3,2,1,0:T(8,128)(2,1)S(1)} custom-call(bf16[4,16,32,128]{3,2,1,0:T(8,128)(2,1)} %bitcast.5, s32[512]{0:T(512)} %chain_s.1, s32[1,512]{1,0:T(1,128)} %bitcast.6, s32[8,8]{1,0:T(8,128)} %block_s.1, f32[5,128]{1,0:T(8,128)} %gains.1, bf16[2,128,640]{2,1,0:T(8,128)(2,1)} %w_in.1, bf16[2,128,128]{2,1,0:T(8,128)(2,1)} %w_out.1, ...), custom_call_target="tpu_custom_call" | custom-call | flops 3000000000 | bytes 2000000 | tf_op jit(solution)/shard_map/triangle_block/pallas_call | solution.py:524
  93.4 0.8 copy.11
